TPU v7x, 512 devices: a whole 4x4x16 slice. The times are simulated.
512 devices in a mesh: branch: 8 (over z_lo), tok: 64 (over y, z_hi, x, core).
Axes of the slice: x: 4, y: 4, z: 16 (z_hi: 2, z_lo: 8; z = z_hi * 8 + z_lo), core: 2. Of those that a mesh axis runs over, the one named last changes fastest.
Arguments:
- teacher_hidden: bfloat16 [8, 1024, 4096], P('branch', 'tok'), may hold values from -400 to 400
- teacher_gain: float32 [8, 4096], P('branch'), may hold values from 0.5 to 1.5
- teacher_head: bfloat16 [8, 4096, 20480], P('branch', None, 'tok'), may hold values from -30 to 30
- student_hidden: bfloat16 [1024, 4096], P('branch'), may hold values from -400 to 400
- student_gain: float32 [4096], replicated, may hold values from 0.5 to 1.5
- student_head: bfloat16 [4096, 20480], P('branch', 'tok'), may hold values from -30 to 30
- cluster_weights: int32 [1024, 8], P(None, 'branch'), may hold values from 0 to 64, as said below
- token_ids: int32 [1024], P('branch'), may hold values from 0 to 20479
Outputs:
- grad_head: float32 [4096, 20480], P('branch', 'tok')
- grad_hidden: float32 [1024, 4096], P('branch', 'tok')
- grad_gain: float32 [4096], P('tok')
Inputs may be any that keep to these rules, and one draw needn't show every extreme that they name: `cluster_weights`: each token's 8 weights sum to 64.
All inputs are finite; a program needn't handle non-finite values.
Results may differ from a plain program's by a relative error of at most 0.0063.
Values may be sent and summed in bfloat16 or wider, within the bound.
A program may use at most 64 MiB of HBM per device.

v0:
```python
import jax
import jax.numpy as jnp
from jax import lax
from jax.sharding import Mesh
from jax.sharding import PartitionSpec as P

DEN = 64
TOK = ("tok_0", "tok_1", "tok_2", "tok_3")
eps = 1e-05
mix_label = 0.25
loss_scale = 64.0


def copy_for_each(value, axis):
    copies = jnp.broadcast_to(value, (lax.axis_size(axis), *value.shape))
    return lax.all_to_all(copies, axis, split_axis=0, concat_axis=0, tiled=True)


def collected_together(value, axis):
    leaves = jax.tree.leaves(value)
    turns = sorted(range(len(leaves)), key=lambda k: -leaves[k].size)
    width = (1, *leaves[turns[0]].shape)[-1]
    lines = [
        jnp.pad(leaves[k].reshape(-1), (0, -leaves[k].size % width)).reshape(-1, width)
        for k in turns
    ]
    both, at, found = (copy_for_each(jnp.concatenate(lines), axis), 0, {})
    for k, line in zip(turns, lines):
        slab = both[:, at : at + len(line)].reshape(len(both), -1)
        found[k] = slab[:, : leaves[k].size].reshape(-1, *leaves[k].shape)
        at += len(line)
    numbers = iter(range(len(leaves)))
    return jax.tree.map(lambda _: found[next(numbers)], value)


def joined_by_halves(pieces, combine):
    while len(jax.tree.leaves(pieces)[0]) > 1:
        pieces = jax.vmap(combine)(
            *(jax.tree.map(lambda part: part[side::2], pieces) for side in (0, 1))
        )
    return jax.tree.map(lambda part: part[0], pieces)


def joined_all(value, axis, combine):
    pieces = collected_together(value, axis)
    return joined_by_halves(pieces, combine)


def cut_along(value, dim, size):
    dims = value.shape
    blocks = value.reshape(*dims[:dim], size, dims[dim] // size, *dims[dim + 1 :])
    return jnp.moveaxis(blocks, dim, 0)


def summed_on_arrival(value, axis, dim):
    blocks = cut_along(value, dim, lax.axis_size(axis))
    arrived = lax.all_to_all(blocks, axis, split_axis=0, concat_axis=0, tiled=True)
    return arrived.sum(axis=0)


def in_order(blocks, dim):
    dims = list(blocks.shape[1:])
    dims[dim] *= blocks.shape[0]
    return jnp.moveaxis(blocks, 0, dim).reshape(dims)


def gathered_copies(value, axis, dim):
    blocks = copy_for_each(value, axis)
    return in_order(blocks, dim)


def summed_rows(value, axes, dim):
    far, near = axes
    blocks = cut_along(value, dim, lax.axis_size(far))
    nearer = summed_on_arrival(blocks, near, dim + 1)
    arrived = lax.all_to_all(nearer, far, split_axis=0, concat_axis=0, tiled=True)
    return arrived.sum(axis=0)


def over_copies(value, axis):
    everything = copy_for_each(value, axis)
    return jnp.sum(everything, axis=0)


def normalize(hidden, gain):
    values = hidden.astype(jnp.float32)
    inv_scale = lax.rsqrt(jnp.mean(values * values, axis=-1, keepdims=True) + eps)
    return ((values * inv_scale * gain).astype(jnp.bfloat16), inv_scale)


def combine_stats(first, second):
    top = jnp.maximum(first[0], second[0])
    return (top, first[1] * jnp.exp(first[0] - top) + second[1] * jnp.exp(second[0] - top))


def probabilities(logits):
    local_max = jnp.max(logits, axis=1)
    local_scaled = jnp.exp(logits - local_max[:, None])
    row_max, row_total = joined_all((local_max, jnp.sum(local_scaled, axis=1)), TOK, combine_stats)
    scaled = local_scaled * jnp.exp(local_max - row_max)[:, None]
    return scaled / row_total[:, None]


def per_device(
    teacher_hidden,
    teacher_gain,
    teacher_head,
    student_hidden,
    student_gain,
    student_head,
    cluster_weights,
    token_ids,
):
    width = student_hidden.shape[1]
    head_cols = teacher_head.shape[2]
    branch_gain = teacher_gain[0]
    branch_head = teacher_head[0]
    normed, unused_scale = normalize(
        lax.all_gather(teacher_hidden[0], TOK, axis=0, tiled=True), branch_gain
    )
    teacher_logits = jnp.dot(normed, branch_head, preferred_element_type=jnp.float32)
    weight = cluster_weights[:, 0].astype(jnp.float32) / DEN
    terms = probabilities(teacher_logits) * weight[:, None]
    mixed = summed_on_arrival(terms, "branch", 0)
    student_normed, inv_scale = normalize(student_hidden, student_gain)
    whole_head = gathered_copies(student_head, "branch", 0)
    student_logits = jnp.dot(student_normed, whole_head, preferred_element_type=jnp.float32)
    student_probs = probabilities(student_logits)
    offset = lax.axis_index(TOK) * head_cols
    onehot = (
        token_ids[:, None] == offset + jnp.arange(head_cols, dtype=jnp.int32)[None, :]
    ).astype(jnp.float32)
    targets = (1.0 - mix_label) * mixed + mix_label * onehot
    logit_grads = (loss_scale * (student_probs - targets)).astype(jnp.bfloat16)
    contract = (((1,), (1,)), ((), ()))
    partial_grads = lax.dot_general(
        logit_grads, whole_head, contract, preferred_element_type=jnp.float32
    )
    normed_grads = summed_rows(partial_grads, (("tok_0", "tok_1", "tok_2"), "tok_3"), 1)
    slice_width = normed_grads.shape[1]
    col_start = lax.axis_index(TOK) * slice_width
    hidden_cols = lax.dynamic_slice_in_dim(student_hidden, col_start, slice_width, 1).astype(
        jnp.float32
    )
    gain_cols = lax.dynamic_slice_in_dim(student_gain, col_start, slice_width, 0)
    grad_gain = over_copies(jnp.sum(normed_grads * hidden_cols * inv_scale, axis=0), "branch")
    row_dots = over_copies(jnp.sum(gain_cols[None, :] * normed_grads * hidden_cols, axis=1), TOK)
    grad_hidden = (
        inv_scale * gain_cols[None, :] * normed_grads
        - hidden_cols * inv_scale**3 * row_dots[:, None] / width
    )
    exchanged = lax.all_to_all(student_normed, "branch", split_axis=1, concat_axis=0, tiled=True)
    all_grads = gathered_copies(logit_grads, "branch", 0)
    grad_head = lax.dot_general(
        exchanged, all_grads, (((0,), (0,)), ((), ())), preferred_element_type=jnp.float32
    )
    return (grad_head, grad_hidden, grad_gain)


def solution(mesh):
    split = Mesh(
        mesh.devices.reshape(mesh.shape["branch"], 4, 2, 4, 2),
        ("branch", "tok_0", "tok_1", "tok_2", "tok_3"),
    )
    in_specs = (
        P("branch", TOK, None),
        P("branch", None),
        P("branch", None, TOK),
        P("branch", None),
        P(),
        P("branch", TOK),
        P(None, "branch"),
        P("branch"),
    )
    out_specs = (P("branch", TOK), P("branch", TOK), P(TOK))
    return jax.shard_map(
        per_device, mesh=split, in_specs=in_specs, out_specs=out_specs, check_vma=False
    )
```

profile of v0, /device:TPU:1, one launch (start us, length us, event | category | flops | bytes accessed | tf_op | source)
XLA Modules:
  0.0 602.1 jit_solution(17609629686330054629)
XLA Ops:
  7.2 0.7 all-gather.3.cloned.1.call-update
  7.9 2.8 broadcast_in_dim.12
  10.7 13.1 %all-to-all-start.1 = ((bf16[8,512,320]{1,2,0:T(8,128)(2,1)}), bf16[8,512,320]{1,2,0:T(8,128)(2,1)}, u32[]{:S(2)}, u32[]{:S(2)}) async-start(bf16[8,512,320]{1,2,0:T(8,128)(2,1)} %broadcast_in_dim.12), calls=%async_computation.1 | async-start | bytes 5242880 | tf_op jit(solution)/shard_map/all_to_all | solution.py:16
  23.8 2.3 copy.51
  26.1 210.6 %all-gather.3.cloned.1.call-done = bf16[1,1024,4096]{2,1,0:T(8,128)(2,1)} async-done(((bf16[1,16,4096]{2,1,0:T(8,128)(2,1)}), bf16[1,1024,4096]{2,1,0:T(8,128)(2,1)}) %all-gather.3.cloned.1.call-update) | async-done | bytes 8388624 | tf_op jit(solution)/shard_map/all_gather | solution.py:119
  236.7 5.2 fusion
  242.0 0.5 copy-done.2
  242.5 3.3 fusion.28
  245.8 1.0 copy-done.3
  247.0 0.9 broadcast_in_dim.14
  248.0 6.0 all-to-all-start.3
  253.9 1.8 fusion.11
  255.7 1.7 fusion.13
  257.5 2.4 copy.69
  259.9 0.9 fusion.29
  260.9 26.4 %all-to-all-done.3 = f32[64,2,1024]{2,1,0:T(2,128)S(1)} async-done(((f32[64,2,1024]{2,1,0:T(2,128)}), f32[64,2,1024]{2,1,0:T(2,128)S(1)}, u32[]{:S(2)}, u32[]{:S(2)}) %all-to-all-start.3) | async-done | bytes 524320 | tf_op jit(solution)/shard_map/all_to_all | solution.py:16
  287.3 0.6 broadcast_in_dim.13
  288.0 7.5 %all-to-all-start.2 = ((f32[64,2,128]{2,1,0:T(2,128)}), f32[64,2,128]{2,1,0:T(2,128)S(1)}, u32[]{:S(2)}, u32[]{:S(2)}) async-start(f32[64,2,128]{2,1,0:T(2,128)} %broadcast_in_dim.13), calls=%async_computation.2 | async-start | bytes 131072 | tf_op jit(solution)/shard_map/all_to_all | solution.py:16
  295.5 0.4 fusion.26
  296.1 0.7 slice.204
  296.8 1.0 multiply_add_fusion
  298.4 2.7 copy_bitcast_fusion.1
  301.1 11.2 %all-to-all-done.2 = f32[64,2,128]{2,1,0:T(2,128)S(1)} async-done(((f32[64,2,128]{2,1,0:T(2,128)}), f32[64,2,128]{2,1,0:T(2,128)S(1)}, u32[]{:S(2)}, u32[]{:S(2)}) %all-to-all-start.2) | async-done | bytes 65568 | tf_op jit(solution)/shard_map/all_to_all | solution.py:16
  312.3 13.7 %all-to-all-start.4 = ((f32[8,128,320]{1,2,0:T(8,128)}), f32[8,128,320]{1,2,0:T(8,128)}, u32[]{:S(2)}, u32[]{:S(2)}) async-start(f32[8,128,320]{1,2,0:T(8,128)} %copy_bitcast_fusion.1), calls=%async_computation.4 | async-start | bytes 2621440 | tf_op jit(solution)/shard_map/all_to_all | solution.py:57
  326.0 2.3 copy.52
  328.2 4.7 copy.53
  332.9 5.3 dot_general.17
  338.8 49.2 %all-to-all-done.4 = f32[8,128,320]{1,2,0:T(8,128)} async-done(((f32[8,128,320]{1,2,0:T(8,128)}), f32[8,128,320]{1,2,0:T(8,128)}, u32[]{:S(2)}, u32[]{:S(2)}) %all-to-all-start.4) | async-done | bytes 1310752 | tf_op jit(solution)/shard_map/all_to_all | solution.py:57
  387.9 1.4 reduce_sum.103
  389.5 3.2 fusion.9
  392.7 0.2 copy.76
  392.9 7.5 %all_to_all.63 = f32[2,32,128,64]{2,3,1,0:T(8,128)} all-to-all(f32[2,32,128,64]{2,3,1,0:T(8,128)S(1)} %bitcast.68), channel_id=1, replica_groups=mesh['branch'=8,'tok_0'=4,'tok_1'=2,'tok_2'=4,'tok_3'=2] {'tok_3'}, dimensions={0} | all-to-all | bytes 4194304 | tf_op jit(solution)/shard_map/all_to_all | solution.py:57
  400.4 4.2 all-to-all-start
  404.7 2.8 reduce_sum.104
  407.5 48.0 %all-to-all-done = bf16[128,8,512]{2,0,1:T(8,128)(2,1)} async-done(((bf16[128,8,512]{2,0,1:T(8,128)(2,1)}), bf16[128,8,512]{2,0,1:T(8,128)(2,1)}, u32[]{:S(2)}, u32[]{:S(2)}) %all-to-all-start) | async-done | bytes 1048608 | tf_op jit(solution)/shard_map/all_to_all | solution.py:152
  455.5 51.6 %all_to_all.64 = f32[32,128,64]{1,2,0:T(8,128)} all-to-all(f32[32,128,64]{1,2,0:T(8,128)} %reduce_sum.104), channel_id=1, replica_groups=mesh['branch'=8,'tok_0'=4,'tok_1'=2,'tok_2'=4,'tok_3'=2] {'tok_0','tok_1..., dimensions={0} | all-to-all | bytes 2097152 | tf_op jit(solution)/shard_map/all_to_all | solution.py:76
  507.0 0.9 broadcast_in_dim.15
  507.9 14.0 %all-to-all-start.5 = ((bf16[8,128,320]{1,2,0:T(8,128)(2,1)}), bf16[8,128,320]{1,2,0:T(8,128)(2,1)S(1)}, u32[]{:S(2)}, u32[]{:S(2)}) async-start(bf16[8,128,320]{1,2,0:T(8,128)(2,1)} %broadcast_in_dim.15), calls=%async_computation.5 | async-start | bytes 1310720 | tf_op jit(solution)/shard_map/all_to_all | solution.py:16
  522.0 1.3 reduce_sum.105
  523.3 0.9 fusion.23
  524.2 21.7 %all-to-all-done.5 = bf16[8,128,320]{1,2,0:T(8,128)(2,1)S(1)} async-done(((bf16[8,128,320]{1,2,0:T(8,128)(2,1)}), bf16[8,128,320]{1,2,0:T(8,128)(2,1)S(1)}, u32[]{:S(2)}, u32[]{:S(2)}) %all-to-all-start.5) | async-done | bytes 655392 | tf_op jit(solution)/shard_map/all_to_all | solution.py:16
  546.0 22.7 %all_to_all.65 = f32[8,1,64]{2,1,0:T(1,128)S(1)} all-to-all(f32[8,1,64]{2,1,0:T(1,128)S(1)} %broadcast_in_dim.17), channel_id=1, replica_groups=mesh['branch'=8,'tok_0'=4,'tok_1'=2,'tok_2'=4,'tok_3'=2] {'branch'}, dimensions={0} | all-to-all | bytes 4096 | tf_op jit(solution)/shard_map/all_to_all | solution.py:16
  568.6 0.6 broadcast_in_dim.16
  569.3 8.1 %all-to-all-start.8 = ((f32[64,1,128]{2,1,0:T(1,128)}), f32[64,1,128]{2,1,0:T(1,128)S(1)}, u32[]{:S(2)}, u32[]{:S(2)}) async-start(f32[64,1,128]{2,1,0:T(1,128)} %broadcast_in_dim.16), calls=%async_computation.8 | async-start | bytes 65536 | tf_op jit(solution)/shard_map/all_to_all | solution.py:16
  577.4 2.6 convolution_bitcast_fusion
  580.0 0.5 reduce_sum.109
  580.5 13.3 %all-to-all-done.8 = f32[64,1,128]{2,1,0:T(1,128)S(1)} async-done(((f32[64,1,128]{2,1,0:T(1,128)}), f32[64,1,128]{2,1,0:T(1,128)S(1)}, u32[]{:S(2)}, u32[]{:S(2)}) %all-to-all-start.8) | async-done | bytes 32800 | tf_op jit(solution)/shard_map/all_to_all | solution.py:16
  593.8 1.4 fusion.20
  (82 shorter events, 1.8 us)
Async XLA Ops:
  7.2 234.8 %copy-start = (bf16[1,4096,320]{1,2,0:T(8,128)(2,1)S(1)}, bf16[1,4096,320]{1,2,0:T(8,128)(2,1)}, u32[]{:S(2)}) copy-start(bf16[1,4096,320]{1,2,0:T(8,128)(2,1)} %param.10) | copy-start | bytes 7864324
  7.2 229.5 %all-gather.3.cloned.1.call-start = ((), (), s32[]{:S(2)}) async-start(), calls=%async_computation.10 | async-start | bytes 8519680 | tf_op jit(solution)/shard_map/all_gather | solution.py:119
  10.7 236.3 %all-to-all-start.1 = ((bf16[8,512,320]{1,2,0:T(8,128)(2,1)}), bf16[8,512,320]{1,2,0:T(8,128)(2,1)}, u32[]{:S(2)}, u32[]{:S(2)}) async-start(bf16[8,512,320]{1,2,0:T(8,128)(2,1)} %broadcast_in_dim.12), calls=%async_computation.1 | async-start | bytes 5242880 | tf_op jit(solution)/shard_map/all_to_all | solution.py:16
  23.8 218.1 %copy-start.7 = (f32[1,4096]{1,0:T(1,128)S(1)}, f32[1,4096]{1,0:T(1,128)}, u32[]{:S(2)}) copy-start(f32[1,4096]{1,0:T(1,128)} %param.9) | copy-start | bytes 49156
  236.7 5.8 copy-start.2
  245.7 1.0 copy-start.3
  245.8 10.0 %copy-start.5 = (s32[1024,1]{0,1:T(1,128)S(1)}, s32[1024,1]{0,1:T(1,128)}, u32[]{:S(2)}) copy-start(s32[1024,1]{0,1:T(1,128)} %param.14) | copy-start | bytes 12292
  245.8 10.0 %copy-start.4 = (f32[4096]{0:T(1024)S(1)}, f32[4096]{0:T(1024)}, u32[]{:S(2)}) copy-start(f32[4096]{0:T(1024)} %param.12) | copy-start | bytes 49156
  248.0 39.4 %all-to-all-start.3 = ((f32[64,2,1024]{2,1,0:T(2,128)}), f32[64,2,1024]{2,1,0:T(2,128)S(1)}, u32[]{:S(2)}, u32[]{:S(2)}) async-start(f32[64,2,1024]{2,1,0:T(2,128)} %broadcast_in_dim.14), calls=%async_computation.3 | async-start | bytes 1048576 | tf_op jit(solution)/shard_map/all_to_all | solution.py:16
  257.5 2.4 copy-start.1
  288.0 24.3 %all-to-all-start.2 = ((f32[64,2,128]{2,1,0:T(2,128)}), f32[64,2,128]{2,1,0:T(2,128)S(1)}, u32[]{:S(2)}, u32[]{:S(2)}) async-start(f32[64,2,128]{2,1,0:T(2,128)} %broadcast_in_dim.13), calls=%async_computation.2 | async-start | bytes 131072 | tf_op jit(solution)/shard_map/all_to_all | solution.py:16
  312.3 75.7 %all-to-all-start.4 = ((f32[8,128,320]{1,2,0:T(8,128)}), f32[8,128,320]{1,2,0:T(8,128)}, u32[]{:S(2)}, u32[]{:S(2)}) async-start(f32[8,128,320]{1,2,0:T(8,128)} %copy_bitcast_fusion.1), calls=%async_computation.4 | async-start | bytes 2621440 | tf_op jit(solution)/shard_map/all_to_all | solution.py:57
  332.9 56.4 %copy-start.6 = (s32[128]{0:T(128)S(1)}, s32[128]{0:T(128)}, u32[]{:S(2)}) copy-start(s32[128]{0:T(128)} %param.15) | copy-start | bytes 1540
  400.4 55.1 %all-to-all-start = ((bf16[128,8,512]{2,0,1:T(8,128)(2,1)}), bf16[128,8,512]{2,0,1:T(8,128)(2,1)}, u32[]{:S(2)}, u32[]{:S(2)}) async-start(bf16[128,8,512]{2,0,1:T(8,128)(2,1)} %copy.52), calls=%async_computation | async-start | bytes 2097152 | tf_op jit(solution)/shard_map/all_to_all | solution.py:152
  507.9 38.0 %all-to-all-start.5 = ((bf16[8,128,320]{1,2,0:T(8,128)(2,1)}), bf16[8,128,320]{1,2,0:T(8,128)(2,1)S(1)}, u32[]{:S(2)}, u32[]{:S(2)}) async-start(bf16[8,128,320]{1,2,0:T(8,128)(2,1)} %broadcast_in_dim.15), calls=%async_computation.5 | async-start | bytes 1310720 | tf_op jit(solution)/shard_map/all_to_all | solution.py:16
  569.3 24.6 %all-to-all-start.8 = ((f32[64,1,128]{2,1,0:T(1,128)}), f32[64,1,128]{2,1,0:T(1,128)S(1)}, u32[]{:S(2)}, u32[]{:S(2)}) async-start(f32[64,1,128]{2,1,0:T(1,128)} %broadcast_in_dim.16), calls=%async_computation.8 | async-start | bytes 65536 | tf_op jit(solution)/shard_map/all_to_all | solution.py:16
Sparse Core Ops, SparseCore 0:
  12.6 224.0 all-gather.2
where the time goes:
time: 603 us; the launch traced here: 602 us
  waiting for transfers between devices  381 us (63%)
  blocking collectives  81.7 us (14%)
  starting transfers between devices  66.6 us (11%)
  local copies, waits for them, and re-layouts  26.8 us (4%)
  other arithmetic  21.5 us (4%)
  between operations  14.4 us (2%)
  matrix products  9.89 us (2%)
    all_gather x1, waiting for transfers between devices, per_device(): lax.all_gather(teacher_hidden[0], TOK, axis=0, tiled=True)  211 us
    all_to_all x5, waiting for transfers between devices, copy_for_each(): return lax.all_to_all(copies, axis, split_axis=0, concat_axis=0, tiled=True)  72.7 us
    all_to_all x1, blocking collectives, summed_rows(): lax.all_to_all(nearer, far, split_axis=0, concat_axis=0, tiled=True)  51.6 us
    all_to_all x1, waiting for transfers between devices, summed_on_arrival(): lax.all_to_all(blocks, axis, split_axis=0, concat_axis=0, tiled=True)  49.2 us
    all_to_all x5, starting transfers between devices, copy_for_each(): return lax.all_to_all(copies, axis, split_axis=0, concat_axis=0, tiled=True)  48.7 us
    all_to_all x1, waiting for transfers between devices, per_device(): lax.all_to_all(student_normed, 'branch', split_axis=1, concat_axis=0, til...  48 us
    all_to_all x1, blocking collectives, copy_for_each(): return lax.all_to_all(copies, axis, split_axis=0, concat_axis=0, tiled=True)  22.7 us
    all_to_all x1, starting transfers between devices, summed_on_arrival(): lax.all_to_all(blocks, axis, split_axis=0, concat_axis=0, tiled=True)  13.7 us
  transfers between devices with their start and end apart: 8, of which 7 were waited for; matrix products, arithmetic and copies ran while one was open for 8% of the time, Pallas kernels for 0%

commit v1 on v0

--- a/solution.py
+++ b/solution.py
@@ -116,7 +116,10 @@
     branch_gain = teacher_gain[0]
     branch_head = teacher_head[0]
     normed, unused_scale = normalize(
-        lax.all_gather(teacher_hidden[0], TOK, axis=0, tiled=True), branch_gain
+        jnp.concatenate(
+            lax.all_to_all(jnp.stack([teacher_hidden[0]] * lax.axis_size(TOK)), TOK, 0, 0), axis=0
+        ),
+        branch_gain,
     )
     teacher_logits = jnp.dot(normed, branch_head, preferred_element_type=jnp.float32)
     weight = cluster_weights[:, 0].astype(jnp.float32) / DEN

time: 603 us -> 867 us (1.44)
  blocking collectives: 81.7 us -> 365 us
  waiting for transfers between devices: 381 us -> 256 us
  starting transfers between devices: 66.6 us -> 173 us
  between operations: 14.4 us -> 1.04 us
  other arithmetic: 21.5 us -> 31.7 us
    all_to_all x0 -> x1, blocking collectives: none -> 283 us  [per_device(): lax.all_to_all(jnp.stack([teacher_hidden[0]] * lax.axis_size(TOK)), TOK,...]
    all_gather x1 -> x0, waiting for transfers between devices: 211 us -> none  [per_device(): lax.all_gather(teacher_hidden[0], TOK, axis=0, tiled=True)]
    all_to_all x5, starting transfers between devices: 48.7 us -> 162 us  [copy_for_each(): return lax.all_to_all(copies, axis, split_axis=0, concat_axis=0, tiled=True)]
    all_to_all x5, waiting for transfers between devices: 72.7 us -> 159 us  [copy_for_each(): return lax.all_to_all(copies, axis, split_axis=0, concat_axis=0, tiled=True)]
    convert_element_type x1 -> x2, other arithmetic: 1.75 us -> 12.1 us  [normalize(): return ((values * inv_scale * gain).astype(jnp.bfloat16), inv_scale)]
  transfers between devices with their start and end apart: 8 -> 7, of which waited for: 7 -> 7; matrix products, arithmetic and copies ran while one was open for 8% -> 7% of each run, Pallas kernels for 0% -> 0%
where the time goes in v1:
time: 867 us; the launch traced here: 866 us
  blocking collectives  365 us (42%)
  waiting for transfers between devices  256 us (30%)
  starting transfers between devices  173 us (20%)
  other arithmetic  31.7 us (4%)
  local copies, waits for them, and re-layouts  27.4 us (3%)
  matrix products  12 us (1%)
    all_to_all x1, blocking collectives, per_device(): lax.all_to_all(jnp.stack([teacher_hidden[0]] * lax.axis_size(TOK)), TOK,...  283 us
    all_to_all x5, starting transfers between devices, copy_for_each(): return lax.all_to_all(copies, axis, split_axis=0, concat_axis=0, tiled=True)  162 us
    all_to_all x5, waiting for transfers between devices, copy_for_each(): return lax.all_to_all(copies, axis, split_axis=0, concat_axis=0, tiled=True)  159 us
    all_to_all x1, blocking collectives, summed_rows(): lax.all_to_all(nearer, far, split_axis=0, concat_axis=0, tiled=True)  51.5 us
    all_to_all x1, waiting for transfers between devices, summed_on_arrival(): lax.all_to_all(blocks, axis, split_axis=0, concat_axis=0, tiled=True)  49.2 us
    all_to_all x1, waiting for transfers between devices, per_device(): lax.all_to_all(student_normed, 'branch', split_axis=1, concat_axis=0, til...  48 us
    all_to_all x1, blocking collectives, copy_for_each(): return lax.all_to_all(copies, axis, split_axis=0, concat_axis=0, tiled=True)  22.7 us
  transfers between devices with their start and end apart: 7, of which 7 were waited for; matrix products, arithmetic and copies ran while one was open for 7% of the time, Pallas kernels for 0%

profile of v1, /device:TPU:1, one launch (start us, length us, event | category | flops | bytes accessed | tf_op | source)
XLA Modules:
  0.0 865.9 jit_solution(3232462583433828311)
XLA Ops:
  0.6 2.1 stack.3
  2.8 283.2 %all_to_all.68 = bf16[64,16,4096]{2,1,0:T(8,128)(2,1)} all-to-all(bf16[64,16,4096]{2,1,0:T(8,128)(2,1)S(1)} %stack.3), channel_id=1, replica_groups=mesh['branch'=8,'tok_0'=4,'tok_1'=2,'tok_2'=4,'tok_3'=2] {'tok_0','tok_1..., dimensions={0} | all-to-all | bytes 16777216 | tf_op jit(solution)/shard_map/all_to_all | solution.py:120
  286.0 1.8 broadcast_in_dim.12
  287.8 118.8 %all-to-all-start.1 = ((bf16[8,512,320]{1,2,0:T(8,128)(2,1)}), bf16[8,512,320]{1,2,0:T(8,128)(2,1)}, u32[]{:S(2)}, u32[]{:S(2)}) async-start(bf16[8,512,320]{1,2,0:T(8,128)(2,1)} %broadcast_in_dim.12), calls=%async_computation.1 | async-start | bytes 5242880 | tf_op jit(solution)/shard_map/all_to_all | solution.py:16
  406.6 2.3 copy.51
  408.9 5.1 fusion
  414.0 10.3 %fusion.2 = bf16[64,16,4096]{2,1,0:T(8,128)(2,1)} fusion(bf16[64,16,4096]{2,1,0:T(8,128)(2,1)} %all_to_all.68, f32[4096]{0:T(1024)S(1)} %bitcast.71, f32[64,16]{1,0:T(8,128)S(1)} %add_rsqrt_fusion), kind=kLoop, calls=%fused_computation.4 | loop fusion | flops 16777216 | bytes 16797696 | tf_op jit(solution)/shard_map/convert_element_type | solution.py:88
  424.3 5.3 fusion.24
  429.7 1.0 copy-done.2
  431.0 94.1 %all-to-all-done.1 = bf16[8,512,320]{1,2,0:T(8,128)(2,1)} async-done(((bf16[8,512,320]{1,2,0:T(8,128)(2,1)}), bf16[8,512,320]{1,2,0:T(8,128)(2,1)}, u32[]{:S(2)}, u32[]{:S(2)}) %all-to-all-start.1) | async-done | bytes 2621472 | tf_op jit(solution)/shard_map/all_to_all | solution.py:16
  525.1 0.9 broadcast_in_dim.14
  526.0 6.6 all-to-all-start.4
  532.6 1.8 fusion.7
  534.5 1.7 fusion.9
  536.2 2.4 copy.69
  538.7 0.9 fusion.25
  539.6 18.3 %all-to-all-done.4 = f32[64,2,1024]{2,1,0:T(2,128)S(1)} async-done(((f32[64,2,1024]{2,1,0:T(2,128)}), f32[64,2,1024]{2,1,0:T(2,128)S(1)}, u32[]{:S(2)}, u32[]{:S(2)}) %all-to-all-start.4) | async-done | bytes 524320 | tf_op jit(solution)/shard_map/all_to_all | solution.py:16
  557.9 0.6 broadcast_in_dim.13
  558.6 14.0 %all-to-all-start.2 = ((f32[64,2,128]{2,1,0:T(2,128)}), f32[64,2,128]{2,1,0:T(2,128)S(1)}, u32[]{:S(2)}, u32[]{:S(2)}) async-start(f32[64,2,128]{2,1,0:T(2,128)} %broadcast_in_dim.13), calls=%async_computation.2 | async-start | bytes 131072 | tf_op jit(solution)/shard_map/all_to_all | solution.py:16
  572.5 0.4 fusion.22
  573.1 0.7 slice.204
  573.9 1.0 multiply_add_fusion
  575.4 2.7 copy_bitcast_fusion.1
  578.1 11.2 %all-to-all-done.2 = f32[64,2,128]{2,1,0:T(2,128)S(1)} async-done(((f32[64,2,128]{2,1,0:T(2,128)}), f32[64,2,128]{2,1,0:T(2,128)S(1)}, u32[]{:S(2)}, u32[]{:S(2)}) %all-to-all-start.2) | async-done | bytes 65568 | tf_op jit(solution)/shard_map/all_to_all | solution.py:16
  589.3 7.3 all-to-all-start.5
  596.6 2.2 copy.52
  598.9 4.7 copy.53
  603.6 5.3 dot_general.17
  609.4 49.2 %all-to-all-done.5 = f32[8,128,320]{1,2,0:T(8,128)} async-done(((f32[8,128,320]{1,2,0:T(8,128)}), f32[8,128,320]{1,2,0:T(8,128)}, u32[]{:S(2)}, u32[]{:S(2)}) %all-to-all-start.5) | async-done | bytes 1310752 | tf_op jit(solution)/shard_map/all_to_all | solution.py:57
  658.6 1.4 reduce_sum.103
  660.1 3.2 fusion.5
  663.6 7.5 all_to_all.69
  671.1 4.2 all-to-all-start
  675.3 2.8 reduce_sum.104
  678.2 48.0 %all-to-all-done = bf16[128,8,512]{2,0,1:T(8,128)(2,1)} async-done(((bf16[128,8,512]{2,0,1:T(8,128)(2,1)}), bf16[128,8,512]{2,0,1:T(8,128)(2,1)}, u32[]{:S(2)}, u32[]{:S(2)}) %all-to-all-start) | async-done | bytes 1048608 | tf_op jit(solution)/shard_map/all_to_all | solution.py:155
  726.1 51.5 %all_to_all.70 = f32[32,128,64]{1,2,0:T(8,128)} all-to-all(f32[32,128,64]{1,2,0:T(8,128)} %reduce_sum.104), channel_id=1, replica_groups=mesh['branch'=8,'tok_0'=4,'tok_1'=2,'tok_2'=4,'tok_3'=2] {'tok_0','tok_1..., dimensions={0} | all-to-all | bytes 2097152 | tf_op jit(solution)/shard_map/all_to_all | solution.py:76
  777.6 0.9 broadcast_in_dim.15
  778.6 14.0 %all-to-all-start.6 = ((bf16[8,128,320]{1,2,0:T(8,128)(2,1)}), bf16[8,128,320]{1,2,0:T(8,128)(2,1)S(1)}, u32[]{:S(2)}, u32[]{:S(2)}) async-start(bf16[8,128,320]{1,2,0:T(8,128)(2,1)} %broadcast_in_dim.15), calls=%async_computation.6 | async-start | bytes 1310720 | tf_op jit(solution)/shard_map/all_to_all | solution.py:16
  792.7 1.3 reduce_sum.105
  794.0 0.9 fusion.19
  794.9 21.7 %all-to-all-done.6 = bf16[8,128,320]{1,2,0:T(8,128)(2,1)S(1)} async-done(((bf16[8,128,320]{1,2,0:T(8,128)(2,1)}), bf16[8,128,320]{1,2,0:T(8,128)(2,1)S(1)}, u32[]{:S(2)}, u32[]{:S(2)}) %all-to-all-start.6) | async-done | bytes 655392 | tf_op jit(solution)/shard_map/all_to_all | solution.py:16
  816.6 22.7 %all_to_all.71 = f32[8,1,64]{2,1,0:T(1,128)S(1)} all-to-all(f32[8,1,64]{2,1,0:T(1,128)S(1)} %broadcast_in_dim.17), channel_id=1, replica_groups=mesh['branch'=8,'tok_0'=4,'tok_1'=2,'tok_2'=4,'tok_3'=2] {'branch'}, dimensions={0} | all-to-all | bytes 4096 | tf_op jit(solution)/shard_map/all_to_all | solution.py:16
  839.3 0.6 broadcast_in_dim.16
  839.9 8.1 all-to-all-start.9
  848.1 2.6 convolution_bitcast_fusion
  850.6 0.5 reduce_sum.109
  851.1 13.3 %all-to-all-done.9 = f32[64,1,128]{2,1,0:T(1,128)S(1)} async-done(((f32[64,1,128]{2,1,0:T(1,128)}), f32[64,1,128]{2,1,0:T(1,128)S(1)}, u32[]{:S(2)}, u32[]{:S(2)}) %all-to-all-start.9) | async-done | bytes 32800 | tf_op jit(solution)/shard_map/all_to_all | solution.py:16
  864.5 1.4 fusion.16
  (82 shorter events, 2.0 us)
Async XLA Ops:
  0.6 423.7 %copy-start = (bf16[1,4096,320]{1,2,0:T(8,128)(2,1)S(1)}, bf16[1,4096,320]{1,2,0:T(8,128)(2,1)}, u32[]{:S(2)}) copy-start(bf16[1,4096,320]{1,2,0:T(8,128)(2,1)} %param.10) | copy-start | bytes 7864324
  2.7 283.2 %copy-start.3 = (bf16[512,320]{0,1:T(8,128)(2,1)S(1)}, bf16[512,320]{0,1:T(8,128)(2,1)}, u32[]{:S(2)}) copy-start(bf16[512,320]{0,1:T(8,128)(2,1)} %param.13) | copy-start | bytes 983044
  287.8 237.3 %all-to-all-start.1 = ((bf16[8,512,320]{1,2,0:T(8,128)(2,1)}), bf16[8,512,320]{1,2,0:T(8,128)(2,1)}, u32[]{:S(2)}, u32[]{:S(2)}) async-start(bf16[8,512,320]{1,2,0:T(8,128)(2,1)} %broadcast_in_dim.12), calls=%async_computation.1 | async-start | bytes 5242880 | tf_op jit(solution)/shard_map/all_to_all | solution.py:16
  408.9 5.1 copy-start.4
  429.7 1.1 copy-start.2
  429.7 104.7 %copy-start.6 = (s32[1024,1]{0,1:T(1,128)S(1)}, s32[1024,1]{0,1:T(1,128)}, u32[]{:S(2)}) copy-start(s32[1024,1]{0,1:T(1,128)} %param.14) | copy-start | bytes 12292
  429.7 104.7 %copy-start.5 = (f32[4096]{0:T(1024)S(1)}, f32[4096]{0:T(1024)}, u32[]{:S(2)}) copy-start(f32[4096]{0:T(1024)} %param.12) | copy-start | bytes 49156
  526.0 31.9 %all-to-all-start.4 = ((f32[64,2,1024]{2,1,0:T(2,128)}), f32[64,2,1024]{2,1,0:T(2,128)S(1)}, u32[]{:S(2)}, u32[]{:S(2)}) async-start(f32[64,2,1024]{2,1,0:T(2,128)} %broadcast_in_dim.14), calls=%async_computation.4 | async-start | bytes 1048576 | tf_op jit(solution)/shard_map/all_to_all | solution.py:16
  536.2 2.4 copy-start.1
  558.6 30.8 %all-to-all-start.2 = ((f32[64,2,128]{2,1,0:T(2,128)}), f32[64,2,128]{2,1,0:T(2,128)S(1)}, u32[]{:S(2)}, u32[]{:S(2)}) async-start(f32[64,2,128]{2,1,0:T(2,128)} %broadcast_in_dim.13), calls=%async_computation.2 | async-start | bytes 131072 | tf_op jit(solution)/shard_map/all_to_all | solution.py:16
  589.3 69.3 %all-to-all-start.5 = ((f32[8,128,320]{1,2,0:T(8,128)}), f32[8,128,320]{1,2,0:T(8,128)}, u32[]{:S(2)}, u32[]{:S(2)}) async-start(f32[8,128,320]{1,2,0:T(8,128)} %copy_bitcast_fusion.1), calls=%async_computation.5 | async-start | bytes 2621440 | tf_op jit(solution)/shard_map/all_to_all | solution.py:57
  603.6 56.4 %copy-start.7 = (s32[128]{0:T(128)S(1)}, s32[128]{0:T(128)}, u32[]{:S(2)}) copy-start(s32[128]{0:T(128)} %param.15) | copy-start | bytes 1540
  671.1 55.1 %all-to-all-start = ((bf16[128,8,512]{2,0,1:T(8,128)(2,1)}), bf16[128,8,512]{2,0,1:T(8,128)(2,1)}, u32[]{:S(2)}, u32[]{:S(2)}) async-start(bf16[128,8,512]{2,0,1:T(8,128)(2,1)} %copy.52), calls=%async_computation | async-start | bytes 2097152 | tf_op jit(solution)/shard_map/all_to_all | solution.py:155
  778.6 38.1 %all-to-all-start.6 = ((bf16[8,128,320]{1,2,0:T(8,128)(2,1)}), bf16[8,128,320]{1,2,0:T(8,128)(2,1)S(1)}, u32[]{:S(2)}, u32[]{:S(2)}) async-start(bf16[8,128,320]{1,2,0:T(8,128)(2,1)} %broadcast_in_dim.15), calls=%async_computation.6 | async-start | bytes 1310720 | tf_op jit(solution)/shard_map/all_to_all | solution.py:16
  839.9 24.6 %all-to-all-start.9 = ((f32[64,1,128]{2,1,0:T(1,128)}), f32[64,1,128]{2,1,0:T(1,128)S(1)}, u32[]{:S(2)}, u32[]{:S(2)}) async-start(f32[64,1,128]{2,1,0:T(1,128)} %broadcast_in_dim.16), calls=%async_computation.9 | async-start | bytes 65536 | tf_op jit(solution)/shard_map/all_to_all | solution.py:16
